TPU v7x, 32 devices: a whole 2x2x4 slice. The times are simulated.
32 devices in a mesh: row: 2 (over x), col: 4 (over z), depth: 4 (over y, core).
Axes of the slice: x: 2, y: 2, z: 4, core: 2. Of those that a mesh axis runs over, the one named last changes fastest.
Arguments:
- row_blocks: bfloat16 [32, 4, 6, 64, 64], P(('row', 'depth'), 'col'), may hold values from -1.5 to 1.5
- row_positions: int32 [32, 4, 6], P(('row', 'depth'), 'col'), may hold values from 0 to 11, as said below
- row_counts: int32 [32, 4], P(('row', 'depth'), 'col'), may hold values from 1 to 6, as said below
- col_blocks: bfloat16 [4, 128, 6, 64, 64], P('row', ('col', 'depth')), may hold values from -1.5 to 1.5
- col_positions: int32 [4, 128, 6], P('row', ('col', 'depth')), may hold values from 0 to 11, as said below
- col_counts: int32 [4, 128], P('row', ('col', 'depth')), may hold values from 1 to 6, as said below
Outputs:
- square: bfloat16 [2048, 8192], P('row', ('col', 'depth'))
Inputs may be any that keep to these rules, and one draw needn't show every extreme that they name: `row_positions`: the positions listed for one block row and panel are distinct. `row_counts`: in every panel some block row lists exactly 6 blocks. `col_positions`: the positions listed for one block column and panel are distinct. `col_counts`: in every panel some block column lists exactly 6 blocks.
All inputs are finite; a program needn't handle non-finite values.
Results may differ from a plain program's by a relative error of at most 0.001.
Values may be sent and summed in bfloat16 or wider, within the bound.
A program may use at most 64 MiB of HBM per device.

v0:
```python
import jax
import jax.numpy as jnp
from jax import lax
from jax.sharding import PartitionSpec as P

BS = 64
KP = 12


def spread_2(block, axis, owner):
    block = jnp.where(lax.axis_index(axis) == owner, block, jnp.zeros_like(block))
    return lax.psum(block, axis)


def shortened(x):

    def short(part):
        return part.astype(jnp.bfloat16) if part.dtype == jnp.float32 else part

    return jax.tree.map(short, x)


def densify_rows(blocks, positions, counts):
    row_total, slot_total = positions.shape
    live_slot = jnp.arange(slot_total, dtype=jnp.int32)[None, :] < counts[:, None]
    targets = jnp.arange(KP, dtype=jnp.int32)
    onehot = ((positions[:, :, None] == targets[None, None, :]) & live_slot[:, :, None]).astype(
        jnp.bfloat16
    )
    spread = jnp.einsum("rsp,rsab->rapb", onehot, blocks, preferred_element_type=jnp.float32)
    return spread.astype(jnp.bfloat16).reshape(row_total * BS, KP * BS)


def densify_cols(blocks, positions, counts):
    col_total, slot_total = positions.shape
    live_slot = jnp.arange(slot_total, dtype=jnp.int32)[None, :] < counts[:, None]
    targets = jnp.arange(KP, dtype=jnp.int32)
    onehot = ((positions[:, :, None] == targets[None, None, :]) & live_slot[:, :, None]).astype(
        jnp.bfloat16
    )
    spread = jnp.einsum("csp,csab->pacb", onehot, blocks, preferred_element_type=jnp.float32)
    return spread.astype(jnp.bfloat16).reshape(KP * BS, col_total * BS)


def group_slice(arrays, offset):
    return tuple((lax.dynamic_slice_in_dim(item, offset, 1, 0)[0] for item in arrays))


def on_device(row_blocks, row_positions, row_counts, col_blocks, col_positions, col_counts):
    left_blocks = row_blocks[:, 0]
    left_positions = row_positions[:, 0]
    left_counts = row_counts[:, 0]
    grid_rows = lax.axis_size("row")
    grid_cols = lax.axis_size("col")
    layers = lax.axis_size("depth")
    per_row = grid_cols // grid_rows
    out_rows = left_blocks.shape[0] * layers * BS
    out_cols = col_blocks.shape[1] * BS

    def advance(panel_id, partial_value):
        pieces = []
        for layer_num in range(layers):
            received = (
                spread_2(left_blocks, ("col", "depth"), panel_id * layers + layer_num),
                spread_2(left_positions, ("col", "depth"), panel_id * layers + layer_num),
                spread_2(left_counts, ("col", "depth"), panel_id * layers + layer_num),
            )
            pieces.append(densify_rows(received[0], received[1], received[2]))
        left_dense = jnp.concatenate(pieces, axis=0)
        own_group = group_slice((col_blocks, col_positions, col_counts), panel_id % per_row)
        received_cols = jax.tree.map(
            lambda part, own: part.astype(own.dtype),
            jax.tree.map(
                lambda part: spread_2(part, "row", panel_id // per_row), shortened(own_group)
            ),
            own_group,
        )
        right_dense = densify_cols(received_cols[0], received_cols[1], received_cols[2])
        return partial_value + jnp.dot(left_dense, right_dense, preferred_element_type=jnp.float32)

    partial_value = lax.fori_loop(
        0, grid_cols, advance, jnp.zeros((out_rows, out_cols), jnp.float32)
    )
    return partial_value.astype(jnp.bfloat16)


def solution(mesh):
    in_specs = (
        P(("row", "depth"), "col", None, None, None),
        P(("row", "depth"), "col", None),
        P(("row", "depth"), "col"),
        P("row", ("col", "depth"), None, None, None),
        P("row", ("col", "depth"), None),
        P("row", ("col", "depth")),
    )
    out_specs = P("row", ("col", "depth"))
    return jax.shard_map(
        on_device, mesh=mesh, in_specs=in_specs, out_specs=out_specs, check_vma=False
    )
```

profile of v0, /device:TPU:0, one launch (start us, length us, event | category | flops | bytes accessed | tf_op | source)
XLA Modules:
  0.0 659.7 jit_solution(7688272672685221979)
XLA Ops:
  6.5 1.3 copy.33
  7.8 642.3 %while.16 = (s32[]{:T(128)}, f32[1024,512]{1,0:T(8,128)}, bf16[4,6,64,64]{3,1,2,0:T(8,128)(2,1)S(1)}, s32[4,6]{1,0:T(4,128)}, s32[4]{0:T(128)}, /*index=5*/bf16[...) while((s32[]{:T(128)}, f32[1024,512]{1,0:T(8,128)}, ...), condition=%wide.region_16.17_spmd.clone, body=%wide.region_0.16_spmd.clone.sunk | while | flops 829165440 | bytes 36248560 | solution.py:81
  7.9 1.2 constant_dynamic-slice_fusion.5
  9.1 1.5 fusion.75
  10.8 1.4 broadcast_select_fusion.16
  12.4 5.3 all-reduce.6
  17.7 61.3 %all-reduce.8 = (s32[4,6]{1,0:T(4,128)S(1)}, s32[4]{0:T(128)S(1)}, s32[4,6]{1,0:T(4,128)S(1)}, s32[4]{0:T(128)S(1)}, s32[4,6]{1,0:T(4,128)S(1)}, /*index=5*/s32[4]{0:T(128)S(1)}, s32[4,6]{1,0:T(4,128)S(1)}, s32[4]{0:T(128)S(1)}) all-reduce(s32[4,6]{1,0:T(4,128)S(1)} %get-tuple-element.382, ...), channel_id=1, replica_groups=mesh['row'=2,'col'=4,'depth'=4] {'col','depth'}, use_global_device_ids=true, to_apply=%region_11.11 | all-reduce | flops 112 | bytes 896 | tf_op jit(solution)/shard_map/while/body/eval_jaxpr/psum | solution.py:12
  79.2 2.4 convert_bitcast_fusion.2
  81.6 1.0 copy.43
  83.6 72.9 %all-reduce.14.cloned.1.call-done = (bf16[4,6,64,64]{3,1,2,0:T(8,128)(2,1)}, bf16[4,6,64,64]{3,1,2,0:T(8,128)(2,1)}, bf16[4,6,64,64]{3,1,2,0:T(8,128)(2,1)}, bf16[4,6,64,64]{3,1,2,0:T(8,128)(2,1)}) async-done(((bf16[4,6,64,64]{3,1,2,0:T(8,128)(2,1)}, bf16[4,6,64,64]{3,1,2,0:T(8,128)(2,1)}, bf16[4,6,64,64]{3,1,2,0:T(8,128)(2,1)}, bf16[4,6,64,64]{3,1,2,0:T(8,128)(2,1)}), (bf16[4,6,64,64]{3,1,2,0:T(8,128)(2,1)}, ...) | async-done | bytes 786448 | tf_op jit(solution)/shard_map/while/body/eval_jaxpr/psum | solution.py:12
  156.5 1.7 fusion.77
  159.8 1.8 fusion.78
  166.8 3.5 select_add_fusion.2
  170.3 1.2 constant_dynamic-slice_fusion.5
  171.5 1.5 fusion.75
  173.2 1.4 broadcast_select_fusion.16
  174.8 4.3 all-reduce.6
  179.1 58.2 %all-reduce.8 = (s32[4,6]{1,0:T(4,128)S(1)}, s32[4]{0:T(128)S(1)}, s32[4,6]{1,0:T(4,128)S(1)}, s32[4]{0:T(128)S(1)}, s32[4,6]{1,0:T(4,128)S(1)}, /*index=5*/s32[4]{0:T(128)S(1)}, s32[4,6]{1,0:T(4,128)S(1)}, s32[4]{0:T(128)S(1)}) all-reduce(s32[4,6]{1,0:T(4,128)S(1)} %get-tuple-element.382, ...), channel_id=1, replica_groups=mesh['row'=2,'col'=4,'depth'=4] {'col','depth'}, use_global_device_ids=true, to_apply=%region_11.11 | all-reduce | flops 112 | bytes 896 | tf_op jit(solution)/shard_map/while/body/eval_jaxpr/psum | solution.py:12
  237.5 2.4 convert_bitcast_fusion.2
  239.9 1.0 copy.43
  240.9 1.0 reshape.188
  241.9 73.9 %all-reduce.14.cloned.1.call-done = (bf16[4,6,64,64]{3,1,2,0:T(8,128)(2,1)}, bf16[4,6,64,64]{3,1,2,0:T(8,128)(2,1)}, bf16[4,6,64,64]{3,1,2,0:T(8,128)(2,1)}, bf16[4,6,64,64]{3,1,2,0:T(8,128)(2,1)}) async-done(((bf16[4,6,64,64]{3,1,2,0:T(8,128)(2,1)}, bf16[4,6,64,64]{3,1,2,0:T(8,128)(2,1)}, bf16[4,6,64,64]{3,1,2,0:T(8,128)(2,1)}, bf16[4,6,64,64]{3,1,2,0:T(8,128)(2,1)}), (bf16[4,6,64,64]{3,1,2,0:T(8,128)(2,1)}, ...) | async-done | bytes 786448 | tf_op jit(solution)/shard_map/while/body/eval_jaxpr/psum | solution.py:12
  315.7 1.7 fusion.77
  319.0 1.8 fusion.78
  326.1 4.2 select_add_fusion.2
  330.3 1.2 constant_dynamic-slice_fusion.5
  331.5 1.5 fusion.75
  333.1 1.4 broadcast_select_fusion.16
  334.8 4.3 all-reduce.6
  339.1 58.1 %all-reduce.8 = (s32[4,6]{1,0:T(4,128)S(1)}, s32[4]{0:T(128)S(1)}, s32[4,6]{1,0:T(4,128)S(1)}, s32[4]{0:T(128)S(1)}, s32[4,6]{1,0:T(4,128)S(1)}, /*index=5*/s32[4]{0:T(128)S(1)}, s32[4,6]{1,0:T(4,128)S(1)}, s32[4]{0:T(128)S(1)}) all-reduce(s32[4,6]{1,0:T(4,128)S(1)} %get-tuple-element.382, ...), channel_id=1, replica_groups=mesh['row'=2,'col'=4,'depth'=4] {'col','depth'}, use_global_device_ids=true, to_apply=%region_11.11 | all-reduce | flops 112 | bytes 896 | tf_op jit(solution)/shard_map/while/body/eval_jaxpr/psum | solution.py:12
  397.5 2.4 convert_bitcast_fusion.2
  399.9 1.0 copy.43
  401.9 73.6 %all-reduce.14.cloned.1.call-done = (bf16[4,6,64,64]{3,1,2,0:T(8,128)(2,1)}, bf16[4,6,64,64]{3,1,2,0:T(8,128)(2,1)}, bf16[4,6,64,64]{3,1,2,0:T(8,128)(2,1)}, bf16[4,6,64,64]{3,1,2,0:T(8,128)(2,1)}) async-done(((bf16[4,6,64,64]{3,1,2,0:T(8,128)(2,1)}, bf16[4,6,64,64]{3,1,2,0:T(8,128)(2,1)}, bf16[4,6,64,64]{3,1,2,0:T(8,128)(2,1)}, bf16[4,6,64,64]{3,1,2,0:T(8,128)(2,1)}), (bf16[4,6,64,64]{3,1,2,0:T(8,128)(2,1)}, ...) | async-done | bytes 786448 | tf_op jit(solution)/shard_map/while/body/eval_jaxpr/psum | solution.py:12
  475.5 1.7 fusion.77
  478.7 1.8 fusion.78
  485.8 4.2 select_add_fusion.2
  490.0 1.2 constant_dynamic-slice_fusion.5
  491.2 1.5 fusion.75
  492.8 1.4 broadcast_select_fusion.16
  494.5 4.3 all-reduce.6
  498.8 58.0 %all-reduce.8 = (s32[4,6]{1,0:T(4,128)S(1)}, s32[4]{0:T(128)S(1)}, s32[4,6]{1,0:T(4,128)S(1)}, s32[4]{0:T(128)S(1)}, s32[4,6]{1,0:T(4,128)S(1)}, /*index=5*/s32[4]{0:T(128)S(1)}, s32[4,6]{1,0:T(4,128)S(1)}, s32[4]{0:T(128)S(1)}) all-reduce(s32[4,6]{1,0:T(4,128)S(1)} %get-tuple-element.382, ...), channel_id=1, replica_groups=mesh['row'=2,'col'=4,'depth'=4] {'col','depth'}, use_global_device_ids=true, to_apply=%region_11.11 | all-reduce | flops 112 | bytes 896 | tf_op jit(solution)/shard_map/while/body/eval_jaxpr/psum | solution.py:12
  557.0 2.4 convert_bitcast_fusion.2
  559.4 1.0 copy.43
  561.4 74.2 %all-reduce.14.cloned.1.call-done = (bf16[4,6,64,64]{3,1,2,0:T(8,128)(2,1)}, bf16[4,6,64,64]{3,1,2,0:T(8,128)(2,1)}, bf16[4,6,64,64]{3,1,2,0:T(8,128)(2,1)}, bf16[4,6,64,64]{3,1,2,0:T(8,128)(2,1)}) async-done(((bf16[4,6,64,64]{3,1,2,0:T(8,128)(2,1)}, bf16[4,6,64,64]{3,1,2,0:T(8,128)(2,1)}, bf16[4,6,64,64]{3,1,2,0:T(8,128)(2,1)}, bf16[4,6,64,64]{3,1,2,0:T(8,128)(2,1)}), (bf16[4,6,64,64]{3,1,2,0:T(8,128)(2,1)}, ...) | async-done | bytes 786448 | tf_op jit(solution)/shard_map/while/body/eval_jaxpr/psum | solution.py:12
  635.6 1.7 fusion.77
  638.9 1.8 fusion.78
  645.9 4.2 select_add_fusion.2
  650.1 2.7 convert_element_type.83
  (156 shorter events, 31.8 us)
Async XLA Ops:
  7.8 71.4 %all-reduce.12.cloned.1.call-start = ((), (), s32[]{:S(2)}) async-start(), calls=%async_computation | async-start | bytes 2097152 | tf_op jit(solution)/shard_map/while/body/eval_jaxpr/psum | solution.py:12
  10.7 145.8 %all-reduce.14.cloned.1.call-start = ((), (), s32[]{:S(2)}) async-start(), calls=%async_computation.1 | async-start | bytes 4194304 | tf_op jit(solution)/shard_map/while/body/eval_jaxpr/psum | solution.py:12
  10.7 1.5 copy-start.4
  10.7 1.6 copy-start.6
  10.8 1.6 copy-start.3
  10.8 1.6 copy-start.5
  159.8 3.3 copy-start.1
  163.1 2.2 copy-start
  165.3 1.5 copy-start.2
  170.3 67.2 %all-reduce.12.cloned.1.call-start = ((), (), s32[]{:S(2)}) async-start(), calls=%async_computation | async-start | bytes 2097152 | tf_op jit(solution)/shard_map/while/body/eval_jaxpr/psum | solution.py:12
  173.1 142.7 %all-reduce.14.cloned.1.call-start = ((), (), s32[]{:S(2)}) async-start(), calls=%async_computation.1 | async-start | bytes 4194304 | tf_op jit(solution)/shard_map/while/body/eval_jaxpr/psum | solution.py:12
  173.1 1.5 copy-start.4
  173.1 1.6 copy-start.6
  173.1 1.6 copy-start.3
  173.2 1.6 copy-start.5
  319.0 3.3 copy-start.1
  322.3 2.2 copy-start
  324.6 1.5 copy-start.2
  330.3 67.2 %all-reduce.12.cloned.1.call-start = ((), (), s32[]{:S(2)}) async-start(), calls=%async_computation | async-start | bytes 2097152 | tf_op jit(solution)/shard_map/while/body/eval_jaxpr/psum | solution.py:12
  333.0 142.4 %all-reduce.14.cloned.1.call-start = ((), (), s32[]{:S(2)}) async-start(), calls=%async_computation.1 | async-start | bytes 4194304 | tf_op jit(solution)/shard_map/while/body/eval_jaxpr/psum | solution.py:12
  333.1 1.5 copy-start.4
  333.1 1.6 copy-start.6
  333.1 1.6 copy-start.3
  333.1 1.6 copy-start.5
  478.7 3.3 copy-start.1
  482.0 2.2 copy-start
  484.3 1.5 copy-start.2
  490.0 67.0 %all-reduce.12.cloned.1.call-start = ((), (), s32[]{:S(2)}) async-start(), calls=%async_computation | async-start | bytes 2097152 | tf_op jit(solution)/shard_map/while/body/eval_jaxpr/psum | solution.py:12
  492.7 142.9 %all-reduce.14.cloned.1.call-start = ((), (), s32[]{:S(2)}) async-start(), calls=%async_computation.1 | async-start | bytes 4194304 | tf_op jit(solution)/shard_map/while/body/eval_jaxpr/psum | solution.py:12
  492.8 1.5 copy-start.4
  492.8 1.6 copy-start.6
  492.8 1.6 copy-start.3
  492.8 1.6 copy-start.5
  638.9 3.3 copy-start.1
  642.2 2.2 copy-start
  644.4 1.5 copy-start.2
Sparse Core Ops, SparseCore 0:
  10.9 42.7 all-reduce.11
  58.2 98.2 all-reduce.13
  173.4 39.6 all-reduce.11
  217.4 98.2 all-reduce.13
  333.1 39.6 all-reduce.11
  377.2 98.2 all-reduce.13
  493.1 39.6 all-reduce.11
  537.3 98.2 all-reduce.13
where the time goes:
time: 661 us; the launch traced here: 660 us
  waiting for transfers between devices  295 us (45%)
  blocking collectives  254 us (38%)
  matrix products  44.9 us (7%)
  local copies, waits for them, and re-layouts  36.2 us (5%)
  other arithmetic  15.4 us (2%)
  between operations  13.4 us (2%)
    psum x8, waiting for transfers between devices, spread_2(): return lax.psum(block, axis)  295 us
    psum x8, blocking collectives, spread_2(): return lax.psum(block, axis)  254 us
    reshape x32, local copies, waits for them, and re-layouts, densify_rows(): return spread.astype(jnp.bfloat16).reshape(row_total * BS, KP * BS)  21.7 us
    dot_general x16, matrix products, densify_rows(): jnp.einsum('rsp,rsab->rapb', onehot, blocks, preferred_element_type=jnp.f...  19.3 us
    dot_general x4, matrix products, advance(): jnp.dot(left_dense, right_dense, preferred_element_type=jnp.float32)  16 us
  transfers between devices with their start and end apart: 8, of which 4 were waited for; matrix products, arithmetic and copies ran while one was open for 4% of the time, Pallas kernels for 0%

commit v1 on v0

v1 whole, which is shorter than its diff:
```python
import functools

import jax
import jax.numpy as jnp
from jax import lax
from jax.experimental import pallas as pl
from jax.experimental.pallas import tpu as pltpu
from jax.sharding import PartitionSpec as P

KP = 12


def packed(blocks):
    *lead, side, _ = blocks.shape
    half = side // 2
    halves = blocks.reshape(-1, 2, half, side)
    return jnp.concatenate([halves[:, 0], halves[:, 1]], axis=-1)


def slot_table(positions, counts, first, dead):
    lists, slots = positions.shape
    slot = jnp.arange(slots, dtype=jnp.int32)
    live = slot[None, :] < counts[:, None]
    hit = (positions[:, :, None] == jnp.arange(KP, dtype=jnp.int32)[None, None, :]) & live[:, :, None]
    place = first + jnp.arange(lists, dtype=jnp.int32)[:, None] * slots + slot[None, :]
    found = jnp.sum(jnp.where(hit, place[:, :, None] + 1, 0), axis=1)
    return jnp.where(found > 0, found - 1, dead)


def side_by_side(a, b):
    half = a.shape[-1] // 2
    top = jnp.concatenate([a[:, :half], b[:, :half]], axis=1)
    bottom = jnp.concatenate([a[:, half:], b[:, half:]], axis=1)
    return top, bottom


def local_kernel(dims, left_tab, right_tab, left_hbm, right_hbm, out_ref, lbuf, rbuf, ld, rd, sems):
    cols, layers, rl, panels, cl, side = dims
    half = side // 2
    nl, nr = left_hbm.shape[0], right_hbm.shape[0]
    get_left = pltpu.make_async_copy(left_hbm, lbuf.at[pl.ds(0, nl)], sems.at[0])
    get_right = pltpu.make_async_copy(right_hbm, rbuf.at[pl.ds(0, nr)], sems.at[1])
    get_right.start()
    get_left.start()
    lbuf[nl] = jnp.zeros_like(lbuf[nl])
    rbuf[nr] = jnp.zeros_like(rbuf[nr])
    get_right.wait()

    def right_step(step, carry):
        g, p = step // KP, step % KP
        base = pl.multiple_of(step * side, side)
        for jp in range(cl // 2):
            a = rbuf[right_tab[(g * cl + 2 * jp) * KP + p]]
            b = rbuf[right_tab[(g * cl + 2 * jp + 1) * KP + p]]
            top, bottom = side_by_side(a, b)
            rd[pl.ds(base, half), jp * 2 * side : (jp + 1) * 2 * side] = top
            rd[pl.ds(base + half, half), jp * 2 * side : (jp + 1) * 2 * side] = bottom
        return carry

    lax.fori_loop(0, panels * KP, right_step, 0)
    get_left.wait()

    def left_step(row, carry):
        base = pl.multiple_of(row * side, side)
        d, i = row // rl, row % rl
        for c in range(cols):
            tab = ((c * layers + d) * rl + i) * KP
            for q in range(KP // 2):
                a = lbuf[left_tab[tab + 2 * q]]
                b = lbuf[left_tab[tab + 2 * q + 1]]
                top, bottom = side_by_side(a, b)
                at = (c * KP // 2 + q) * 2 * side
                ld[pl.ds(base, half), at : at + 2 * side] = top
                ld[pl.ds(base + half, half), at : at + 2 * side] = bottom
        return carry

    lax.fori_loop(0, layers * rl, left_step, 0)
    tile = 256

    def multiply(m, carry):
        at = pl.ds(pl.multiple_of(m * tile, tile), tile)
        out_ref[at, :] = jnp.dot(ld[at, :], rd[...], preferred_element_type=jnp.float32).astype(jnp.bfloat16)
        return carry

    lax.fori_loop(0, out_ref.shape[0] // tile, multiply, 0)


def on_device(row_blocks, row_positions, row_counts, col_blocks, col_positions, col_counts):
    rows, cols, layers = lax.axis_size("row"), lax.axis_size("col"), lax.axis_size("depth")
    rl, _, slots, side, _ = row_blocks.shape
    pg, cl = col_blocks.shape[:2]
    panels = pg * rows
    nl, nr = cols * layers * rl * slots, panels * cl * slots
    owner = lax.axis_index("col") * layers + lax.axis_index("depth")
    left_tab = slot_table(row_positions[:, 0], row_counts[:, 0], owner * rl * slots, nl)
    right_tab = slot_table(
        col_positions.reshape(pg * cl, slots), col_counts.reshape(pg * cl), lax.axis_index("row") * pg * cl * slots, nr
    )
    left = lax.all_gather(packed(row_blocks), ("col", "depth"), axis=0, tiled=True)
    right = lax.all_gather(packed(col_blocks), "row", axis=0, tiled=True)
    left_tab = lax.all_gather(left_tab.reshape(-1), ("col", "depth"), axis=0, tiled=True)
    right_tab = lax.all_gather(right_tab.reshape(-1), "row", axis=0, tiled=True)
    m, n, k = layers * rl * side, cl * side, panels * KP * side
    half = side // 2
    any_spec = pl.BlockSpec(memory_space=pl.ANY)
    return pl.pallas_call(
        functools.partial(local_kernel, (cols, layers, rl, panels, cl, side)),
        out_shape=jax.ShapeDtypeStruct((m, n), jnp.bfloat16),
        in_specs=[pl.BlockSpec(memory_space=pltpu.SMEM)] * 2 + [any_spec] * 2,
        out_specs=pl.BlockSpec(memory_space=pltpu.VMEM),
        scratch_shapes=[
            pltpu.VMEM((nl + 1, half, 2 * side), jnp.bfloat16),
            pltpu.VMEM((nr + 1, half, 2 * side), jnp.bfloat16),
            pltpu.VMEM((m, k), jnp.bfloat16),
            pltpu.VMEM((k, n), jnp.bfloat16),
            pltpu.SemaphoreType.DMA((2,)),
        ],
        compiler_params=pltpu.CompilerParams(vmem_limit_bytes=48 * 1024 * 1024),
        cost_estimate=pl.CostEstimate(flops=2 * m * n * k, bytes_accessed=2 * (m * n + (nl + nr) * side * side), transcendentals=0),
    )(left_tab, right_tab, left, right)


def solution(mesh):
    in_specs = (
        P(("row", "depth"), "col", None, None, None),
        P(("row", "depth"), "col", None),
        P(("row", "depth"), "col"),
        P("row", ("col", "depth"), None, None, None),
        P("row", ("col", "depth"), None),
        P("row", ("col", "depth")),
    )
    return jax.shard_map(
        on_device, mesh=mesh, in_specs=in_specs, out_specs=P("row", ("col", "depth")), check_vma=False
    )
```

time: 661 us -> 111 us (0.17)
  waiting for transfers between devices: 295 us -> 55.2 us
  blocking collectives: 254 us -> 18 us
  matrix products: 44.9 us -> 0 us
  local copies, waits for them, and re-layouts: 36.2 us -> 7.04 us
  Pallas kernels: 0 us -> 13.4 us
  other arithmetic: 15.4 us -> 2.36 us
    psum x8 -> x0, waiting for transfers between devices: 295 us -> none  [spread_2(): return lax.psum(block, axis)]
    psum x8 -> x0, blocking collectives: 254 us -> none  [spread_2(): return lax.psum(block, axis)]
    all_gather x0 -> x2, waiting for transfers between devices: none -> 55.2 us  [the longest x1 47.5 us: on_device(): lax.all_gather(packed(row_blocks), ('col', 'depth'), axis=0, tiled=True)]
    dot_general x24 -> x0, matrix products: 44.9 us -> none  [the longest x16 19.3 us: densify_rows(): jnp.einsum('rsp,rsab->rapb', onehot, blocks, preferred_element_type=jnp.f...]
    reshape x36 -> x0, local copies, waits for them, and re-layouts: 25.5 us -> none  [the longest x32 21.7 us: densify_rows(): return spread.astype(jnp.bfloat16).reshape(row_total * BS, KP * BS)]
    unnamed x0 -> x2, blocking collectives: none -> 18 us
    pallas_call x0 -> x1, Pallas kernels: none -> 13.4 us  [on_device(): pl.pallas_call(functools.partial(local_kernel, (cols, layers, rl, panels,...]
    select_n x24 -> x2, other arithmetic: 11.9 us -> 0.01 us  [slot_table(): return jnp.where(found > 0, found - 1, dead)]
  transfers between devices with their start and end apart: 8 -> 2, of which waited for: 4 -> 2; matrix products, arithmetic and copies ran while one was open for 4% -> 3% of each run, Pallas kernels for 0% -> 0%
where the time goes in v1:
time: 111 us
  waiting for transfers between devices  55.2 us (50%)
  blocking collectives  18 us (16%)
  between operations  14.7 us (13%)
  Pallas kernels  13.4 us (12%)
  local copies, waits for them, and re-layouts  7.04 us (6%)
  other arithmetic  2.36 us (2%)
    all_gather x1, waiting for transfers between devices, on_device(): lax.all_gather(packed(row_blocks), ('col', 'depth'), axis=0, tiled=True)  47.5 us
    unnamed x2, blocking collectives  18 us
    pallas_call x1, Pallas kernels, on_device(): pl.pallas_call(functools.partial(local_kernel, (cols, layers, rl, panels,...  13.4 us
    all_gather x1, waiting for transfers between devices, on_device(): right = lax.all_gather(packed(col_blocks), 'row', axis=0, tiled=True)  7.66 us
    unnamed x24, local copies, waits for them, and re-layouts  4.94 us
  transfers between devices with their start and end apart: 2, of which 2 were waited for; matrix products, arithmetic and copies ran while one was open for 3% of the time, Pallas kernels for 0%

profile of v1, /device:TPU:0, one launch (start us, length us, event | category | flops | bytes accessed | tf_op | source)
XLA Modules:
  0.0 110.7 jit_solution(10486912764124681335)
XLA Ops:
  6.5 0.0 all-gather.5.cloned.1.call-start
  6.5 1.7 %slice_bitcast_fusion.1 = (bf16[96,32,64]{2,1,0:T(8,128)(2,1)S(1)}, bf16[96,32,64]{2,1,0:T(8,128)(2,1)S(1)}) fusion(bf16[96,2,32,64]{3,2,1,0:T(8,128)(2,1)} %bitcast.20), kind=kLoop, calls=%fused_computation.1 | loop fusion | bytes 1572864 | tf_op jit(solution)/shard_map/squeeze | solution.py:17
  8.2 0.0 copy-start.2
  8.2 1.3 %pad_maximum_fusion = bf16[96,32,128]{2,1,0:T(8,128)(2,1)} fusion(bf16[96,32,64]{2,1,0:T(8,128)(2,1)S(1)} %get-tuple-element.6, bf16[96,32,64]{2,1,0:T(8,128)(2,1)S(1)} %get-tuple-element.5), kind=kLoop, calls=%fused_computation.2 | loop fusion | flops 1572864 | bytes 1572864 | tf_op jit(solution)/shard_map/concatenate | solution.py:17
  9.5 0.0 copy-start.8
  9.5 0.0 copy-start.7
  9.5 0.0 copy-start.5
  9.5 0.0 copy-start.4
  9.5 0.0 copy-start.6
  9.6 0.0 copy-start.3
  9.6 0.0 all-gather.5.cloned.1.call-update
  9.6 0.0 all-gather.3.cloned.1.call-start
  9.6 0.0 copy-done.2
  9.7 0.8 pad_maximum_fusion.1
  10.5 0.0 all-gather.3.cloned.1.call-update
  10.5 0.0 copy-done.8
  10.5 0.6 dynamic-slice.1
  11.1 0.0 copy-done.7
  11.1 0.6 dynamic-slice
  11.7 0.0 copy-done.5
  11.7 0.1 lt.45
  11.8 0.0 copy-done.4
  11.8 0.1 copy.16
  11.9 0.0 copy-done.6
  11.9 0.1 select_reduce_fusion.1
  12.0 0.1 reshape.130
  12.1 0.0 copy-done.3
  12.1 0.1 eq.34
  12.2 0.1 select_reduce_fusion
  12.3 0.1 reshape.133
  13.5 0.2 dynamic-update-slice.1
  13.8 0.2 dynamic-update-slice
  14.0 5.2 %all-reduce.1.right_tab = s32[384]{0:T(512)S(1)} all-reduce(s32[384]{0:T(512)S(1)} %dynamic-update-slice.1), channel_id=1, replica_groups=mesh['row'=2,'col'=4,'depth'=4] {'row'}, use_global_device_ids=true, to_apply=%add.1 | all-reduce | flops 384 | bytes 3072
  19.2 12.8 %all-reduce.left_tab = s32[768]{0:T(1024)S(1)} all-reduce(s32[768]{0:T(1024)S(1)} %dynamic-update-slice), channel_id=1, replica_groups=mesh['row'=2,'col'=4,'depth'=4] {'col','depth'}, use_global_device_ids=true, to_apply=%add | all-reduce | flops 768 | bytes 6144
  32.0 7.7 %all-gather.5.cloned.1.call-done.right_hbm = bf16[192,32,128]{2,1,0:T(8,128)(2,1)} async-done(((bf16[96,32,128]{2,1,0:T(8,128)(2,1)}), bf16[192,32,128]{2,1,0:T(8,128)(2,1)}) %all-gather.5.cloned.1.call-update) | async-done | bytes 1572880 | tf_op jit(solution)/shard_map/all_gather | solution.py:100
  39.6 47.5 %all-gather.3.cloned.1.call-done.left_hbm = bf16[384,32,128]{2,1,0:T(8,128)(2,1)} async-done(((bf16[24,32,128]{2,1,0:T(8,128)(2,1)}), bf16[384,32,128]{2,1,0:T(8,128)(2,1)}) %all-gather.3.cloned.1.call-update) | async-done | bytes 3145744 | tf_op jit(solution)/shard_map/all_gather | solution.py:99
  87.2 0.0 copy-start
  87.2 1.9 %copy-done = bf16[384,32,128]{2,1,0:T(8,128)(2,1)S(1)} copy-done((bf16[384,32,128]{2,1,0:T(8,128)(2,1)S(1)}, bf16[384,32,128]{2,1,0:T(8,128)(2,1)}, u32[]{:S(2)}) %copy-start) | copy-done | bytes 3145752
  89.1 0.0 copy-start.1
  89.1 1.4 %copy-done.1 = bf16[192,32,128]{2,1,0:T(8,128)(2,1)S(1)} copy-done((bf16[192,32,128]{2,1,0:T(8,128)(2,1)S(1)}, bf16[192,32,128]{2,1,0:T(8,128)(2,1)}, u32[]{:S(2)}) %copy-start.1) | copy-done | bytes 1572888
  90.5 13.4 %shard_map.67 = bf16[1024,512]{1,0:T(8,128)(2,1)} custom-call(s32[768]{0:T(1024)S(1)} %all-reduce.left_tab, s32[384]{0:T(512)S(1)} %all-reduce.1.right_tab, bf16[384,32,128]{2,1,0:T(8,128)(2,1)S(1)} %copy-done, bf16[192,32,128]{2,1,0:T(8,128)(2,1)S(1)} %copy-done.1), custom_call_target="tpu_custom_call" | custom-call | flops 3221225472 | bytes 5767168 | tf_op jit(solution)/shard_map/pallas_call | solution.py:106
  (11 shorter events, 0.1 us)
Async XLA Ops:
  6.5 33.1 %all-gather.5.cloned.1.call-start = ((), (), s32[]{:S(2)}) async-start(), calls=%async_computation.1 | async-start | bytes 2359296 | tf_op jit(solution)/shard_map/all_gather | solution.py:100
  8.2 1.4 %copy-start.2 = (bf16[4,1,6,64,64]{4,3,2,1,0:T(8,128)(2,1)S(1)}, bf16[4,1,6,64,64]{4,3,2,1,0:T(8,128)(2,1)}, u32[]{:S(2)}) copy-start(bf16[4,1,6,64,64]{4,3,2,1,0:T(8,128)(2,1)} %param.6) | copy-start | bytes 589828
  9.5 1.0 copy-start.8
  9.5 1.6 %copy-start.7 = (u32[32]{0:T(128)S(1)}, u32[32]{0:T(128)}, u32[]{:S(2)}) copy-start(u32[32]{0:T(128)} %constant.50) | copy-start | bytes 388
  9.5 2.2 %copy-start.5 = (s32[2,8]{1,0:T(2,128)S(1)}, s32[2,8]{1,0:T(2,128)}, u32[]{:S(2)}) copy-start(s32[2,8]{1,0:T(2,128)} %param.11) | copy-start | bytes 196
  9.5 2.2 %copy-start.4 = (s32[4,1,6]{2,1,0:T(1,128)S(1)}, s32[4,1,6]{2,1,0:T(1,128)}, u32[]{:S(2)}) copy-start(s32[4,1,6]{2,1,0:T(1,128)} %param.7) | copy-start | bytes 292
  9.5 2.3 %copy-start.6 = (s32[4,1]{0,1:T(1,128)S(1)}, s32[4,1]{0,1:T(1,128)}, u32[]{:S(2)}) copy-start(s32[4,1]{0,1:T(1,128)} %param.8) | copy-start | bytes 52
  9.6 2.5 %copy-start.3 = (s32[2,8,6]{1,0,2:T(2,128)S(1)}, s32[2,8,6]{1,0,2:T(2,128)}, u32[]{:S(2)}) copy-start(s32[2,8,6]{1,0,2:T(2,128)} %param.10) | copy-start | bytes 1156
  9.6 77.6 %all-gather.3.cloned.1.call-start = ((), (), s32[]{:S(2)}) async-start(), calls=%async_computation | async-start | bytes 3342336 | tf_op jit(solution)/shard_map/all_gather | solution.py:99
  87.2 1.9 %copy-start = (bf16[384,32,128]{2,1,0:T(8,128)(2,1)S(1)}, bf16[384,32,128]{2,1,0:T(8,128)(2,1)}, u32[]{:S(2)}) copy-start(bf16[384,32,128]{2,1,0:T(8,128)(2,1)} %all-gather.3.cloned.1.call-done.left_hbm) | copy-start | bytes 9437188
  89.1 1.4 %copy-start.1 = (bf16[192,32,128]{2,1,0:T(8,128)(2,1)S(1)}, bf16[192,32,128]{2,1,0:T(8,128)(2,1)}, u32[]{:S(2)}) copy-start(bf16[192,32,128]{2,1,0:T(8,128)(2,1)} %all-gather.5.cloned.1.call-done.right_hbm) | copy-start | bytes 4718596
Sparse Core Ops, SparseCore 0:
  9.7 29.8 all-gather.4
  41.9 45.1 all-gather.2

commit v2 on v1

v2 whole, which is shorter than its diff:
```python
import functools

import jax
import jax.numpy as jnp
from jax import lax
from jax.experimental import pallas as pl
from jax.experimental.pallas import tpu as pltpu
from jax.sharding import PartitionSpec as P

KP = 12
MESH = pl.DeviceIdType.MESH
TAB = 16


def slot_table(positions, counts):
    slots = positions.shape[-1]
    slot = jnp.arange(slots, dtype=jnp.int32)
    live = slot < counts[..., None]
    hit = (positions[..., :, None] == jnp.arange(KP, dtype=jnp.int32)) & live[..., :, None]
    found = jnp.sum(jnp.where(hit, slot[:, None] + 1, 0), axis=-2)
    return found.astype(jnp.bfloat16)


def partner(index, bit):
    return index + bit - 2 * bit * ((index // bit) % 2)


def bits_of(size):
    bits = []
    while size > 1:
        size //= 2
        bits.append(size)
    return bits


def moved(index, e, bits):
    for bit in bits:
        if e & bit:
            index = partner(index, bit)
    return index


def lower_bits(e, bits):
    return [n for n, bit in enumerate(bits) if e == 0 or bit < (e & -e)]


def placed(tab, row, parts):
    want = jnp.broadcast_to(tab[row : row + 1, :], (TAB, tab.shape[1]))
    outs = [jnp.zeros_like(part) for part in parts[0]]
    for s, part in enumerate(parts):
        mask = want == jnp.asarray(s + 1, tab.dtype)
        outs = [jnp.where(mask, new, old) for new, old in zip(part, outs)]
    return outs


def kernel(dims, lblk, ltab, rblk, rtab, out_ref, lbuf, rbuf, ld, rd, lsend, lrecv, rsend, rrecv):
    rows, cols, layers, rl, pg, cl, slots, side = dims
    half = side // 2
    width = 2 * side
    r, c, d = lax.axis_index("row"), lax.axis_index("col"), lax.axis_index("depth")
    lbits, rbits = bits_of(layers), bits_of(rows)
    chunks = pg * cl // 2
    me = c * layers + d

    barrier = pltpu.get_barrier_semaphore()
    peers = [{"depth": partner(d, bit)} for bit in lbits] + [{"row": partner(r, bit)} for bit in rbits]
    if cols > 1:
        peers += [{"col": lax.rem(c + 1, cols)}, {"col": lax.rem(c + cols - 1, cols)}]
    for peer in peers:
        pl.semaphore_signal(barrier, inc=1, device_id=peer, device_id_type=MESH)

    def pack_left(i, carry):
        for s in range(slots):
            x = lblk[i, s]
            lbuf[me, i, s * half : (s + 1) * half, :] = jnp.concatenate([x[:half], x[half:]], axis=1)
        lbuf[me, i, slots * half : slots * half + TAB, :] = ltab[i]
        return carry

    lax.fori_loop(0, rl, pack_left, 0)
    pl.semaphore_wait(barrier, len(peers))

    def left_copy(way, owner, device):
        return pltpu.make_async_remote_copy(
            src_ref=lbuf.at[owner],
            dst_ref=lbuf.at[owner],
            send_sem=lsend.at[way, owner],
            recv_sem=lrecv.at[owner],
            device_id=device,
            device_id_type=MESH,
        )

    def left_sends(t, side_of, e, act):
        src = c + t if side_of else c - t
        owner = src * layers + moved(d, e, lbits)
        if e == 0:
            if side_of == 0:
                @pl.when(c + 1 < cols)
                def _():
                    act(left_copy(0, owner, {"col": c + 1}))

            def to_lower():
                act(left_copy(1, owner, {"col": c - 1}))

            if side_of == 1:
                pl.when(c > 0)(to_lower)
            else:
                pl.when((c > 0) & (t == 0))(to_lower)
        for n in lower_bits(e, lbits):
            act(left_copy(2 + n, owner, {"depth": partner(d, lbits[n])}))

    def valid(t, side_of):
        if side_of:
            return (t > 0) & (c + t < cols)
        return (t >= 0) & (c - t >= 0)

    left_sends(0, 0, 0, lambda copy: copy.start())

    def right_copy(n, owner, chunk):
        return pltpu.make_async_remote_copy(
            src_ref=rbuf.at[owner, chunk],
            dst_ref=rbuf.at[owner, chunk],
            send_sem=rsend.at[n, owner, chunk],
            recv_sem=rrecv.at[owner, chunk],
            device_id={"row": partner(r, rbits[n])},
            device_id_type=MESH,
        )

    def pack_right(chunk, carry):
        for s in range(slots):
            rbuf[r, chunk, s * side : (s + 1) * side, :] = jnp.concatenate(
                [rblk[2 * chunk, s], rblk[2 * chunk + 1, s]], axis=1
            )
        rbuf[r, chunk, slots * side : slots * side + TAB, :] = rtab[chunk]
        for n in lower_bits(0, rbits):
            right_copy(n, r, chunk).start()
        return carry

    lax.fori_loop(0, chunks, pack_right, 0)

    def place_right(owner, chunk):
        g = owner * pg + chunk // (cl // 2)
        lanes = pl.ds(pl.multiple_of((chunk % (cl // 2)) * width, width), width)
        tab = rbuf[owner, chunk, slots * side : slots * side + TAB, :]
        for v in range(side // TAB):
            parts = [(rbuf[owner, chunk, s * side + v * TAB : s * side + (v + 1) * TAB, :],) for s in range(slots)]
            for p in range(KP):
                (block,) = placed(tab, p, parts)
                rd[pl.ds(pl.multiple_of((g * KP + p) * side + v * TAB, TAB), TAB), lanes] = block

    def place_left(src, layer):
        owner = src * layers + layer

        def one(i, carry):
            base = (layer * rl + i) * side
            tab = lbuf[owner, i, slots * half : slots * half + TAB, :]
            for v in range(half // TAB):
                parts = []
                for s in range(slots):
                    x = lbuf[owner, i, s * half + v * TAB : s * half + (v + 1) * TAB, :]
                    lo, hi = x[:, :side], x[:, side:]
                    parts.append((jnp.concatenate([lo, lo], axis=1), jnp.concatenate([hi, hi], axis=1)))
                for q in range(KP // 2):
                    top, bottom = placed(tab, q, parts)
                    lanes = pl.ds(pl.multiple_of((src * (KP // 2) + q) * width, width), width)
                    ld[pl.ds(pl.multiple_of(base + v * TAB, TAB), TAB), lanes] = top
                    ld[pl.ds(pl.multiple_of(base + half + v * TAB, TAB), TAB), lanes] = bottom
            return carry

        lax.fori_loop(0, rl, one, 0)

    def own_right(chunk, carry):
        place_right(r, chunk)
        return carry

    lax.fori_loop(0, chunks, own_right, 0)

    order = sorted(range(layers), key=lambda e: (e.bit_count(), -e))
    last = max(e.bit_count() for e in order)

    def left_step(t, carry):
        for e in order:
            lag = e.bit_count()
            for side_of in (0, 1):
                tt = t - lag

                @pl.when(valid(tt, side_of) & (tt < cols))
                def _(tt=tt, e=e, side_of=side_of):
                    src = c + tt if side_of else c - tt
                    layer = moved(d, e, lbits)

                    def arrive():
                        left_copy(0, src * layers + layer, {"depth": partner(d, 1)}).wait_recv()
                        left_sends(tt, side_of, e, lambda copy: copy.start())

                    if e == 0:
                        pl.when(tt > 0)(arrive)
                    else:
                        arrive()
                    place_left(src, layer)
        return carry

    lax.fori_loop(0, cols + last, left_step, 0)

    for e in sorted(range(1, rows), key=lambda e: (e.bit_count(), -e)):
        owner = moved(r, e, rbits)

        def right_step(chunk, carry, owner=owner, e=e):
            right_copy(0, owner, chunk).wait_recv()
            for n in lower_bits(e, rbits):
                right_copy(n, owner, chunk).start()
            place_right(owner, chunk)
            return carry

        lax.fori_loop(0, chunks, right_step, 0)

    tile = 256

    def multiply(m, carry):
        at = pl.ds(pl.multiple_of(m * tile, tile), tile)
        out_ref[at, :] = jnp.dot(ld[at, :], rd[...], preferred_element_type=jnp.float32).astype(jnp.bfloat16)
        return carry

    lax.fori_loop(0, out_ref.shape[0] // tile, multiply, 0)

    def left_done(t, carry):
        for e in range(layers):
            for side_of in (0, 1):

                @pl.when(valid(t, side_of))
                def _(e=e, side_of=side_of):
                    left_sends(t, side_of, e, lambda copy: copy.wait_send())

        return carry

    lax.fori_loop(0, cols, left_done, 0)
    for e in range(rows):
        owner = moved(r, e, rbits)

        def right_done(chunk, carry, owner=owner, e=e):
            for n in lower_bits(e, rbits):
                right_copy(n, owner, chunk).wait_send()
            return carry

        lax.fori_loop(0, chunks, right_done, 0)


def lane_pairs(pairs, side):
    wide = jnp.repeat(pairs, side, axis=-1)
    return jnp.pad(wide, [(0, 0)] * (wide.ndim - 2) + [(0, TAB - wide.shape[-2]), (0, 0)])


def on_device(row_blocks, row_positions, row_counts, col_blocks, col_positions, col_counts):
    rows, cols, layers = lax.axis_size("row"), lax.axis_size("col"), lax.axis_size("depth")
    rl, _, slots, side, _ = row_blocks.shape
    pg, cl = col_blocks.shape[:2]
    panels = pg * rows
    chunks = pg * cl // 2
    left_tab = slot_table(row_positions[:, 0], row_counts[:, 0])
    left_tab = lane_pairs(left_tab.reshape(rl, KP // 2, 2), side)
    right_tab = slot_table(col_positions, col_counts).reshape(chunks, 2, KP)
    right_tab = lane_pairs(right_tab.transpose(0, 2, 1), side)
    m, n, k = layers * rl * side, cl * side, panels * KP * side
    width = 2 * side
    vmem = pl.BlockSpec(memory_space=pltpu.VMEM)
    return pl.pallas_call(
        functools.partial(kernel, (rows, cols, layers, rl, pg, cl, slots, side)),
        out_shape=jax.ShapeDtypeStruct((m, n), jnp.bfloat16),
        in_specs=[vmem] * 4,
        out_specs=vmem,
        scratch_shapes=[
            pltpu.VMEM((cols * layers, rl, slots * side // 2 + TAB, width), jnp.bfloat16),
            pltpu.VMEM((rows, chunks, slots * side + TAB, width), jnp.bfloat16),
            pltpu.VMEM((m, k), jnp.bfloat16),
            pltpu.VMEM((k, n), jnp.bfloat16),
            pltpu.SemaphoreType.DMA((2 + len(bits_of(layers)), cols * layers)),
            pltpu.SemaphoreType.DMA((cols * layers,)),
            pltpu.SemaphoreType.DMA((len(bits_of(rows)), rows, chunks)),
            pltpu.SemaphoreType.DMA((rows, chunks)),
        ],
        compiler_params=pltpu.CompilerParams(
            collective_id=0, has_side_effects=True, vmem_limit_bytes=48 * 1024 * 1024
        ),
        cost_estimate=pl.CostEstimate(flops=2 * m * n * k, bytes_accessed=2 * m * n, transcendentals=0),
    )(row_blocks[:, 0], left_tab, col_blocks.reshape(pg * cl, slots, side, side), right_tab)


def solution(mesh):
    in_specs = (
        P(("row", "depth"), "col", None, None, None),
        P(("row", "depth"), "col", None),
        P(("row", "depth"), "col"),
        P("row", ("col", "depth"), None, None, None),
        P("row", ("col", "depth"), None),
        P("row", ("col", "depth")),
    )
    return jax.shard_map(
        on_device, mesh=mesh, in_specs=in_specs, out_specs=P("row", ("col", "depth")), check_vma=False
    )
```

time: 111 us -> 42.8 us (0.39)
  waiting for transfers between devices: 55.2 us -> 0 us
  Pallas kernels: 13.4 us -> 35.3 us
  blocking collectives: 18 us -> 0 us
  between operations: 14.7 us -> 0.08 us
  local copies, waits for them, and re-layouts: 7.04 us -> 5.55 us
    all_gather x2 -> x0, waiting for transfers between devices: 55.2 us -> none  [the longest x1 47.5 us: on_device(): lax.all_gather(packed(row_blocks), ('col', 'depth'), axis=0, tiled=True)]
    pallas_call x1, Pallas kernels: 13.4 us -> 35.3 us  [on_device(): pl.pallas_call(functools.partial(kernel, (rows, cols, layers, rl, pg, cl,...]
    unnamed x2 -> x0, blocking collectives: 18 us -> none
    concatenate x2 -> x0, other arithmetic: 2.12 us -> none  [packed(): return jnp.concatenate([halves[:, 0], halves[:, 1]], axis=-1)]
    squeeze x2 -> x0, local copies, waits for them, and re-layouts: 1.69 us -> none  [packed(): return jnp.concatenate([halves[:, 0], halves[:, 1]], axis=-1)]
    lt x2, other arithmetic: 0.01 us -> 1.34 us  [slot_table(): live = slot < counts[..., None]]
    unnamed x24 -> x6, local copies, waits for them, and re-layouts: 4.94 us -> 4.07 us
  transfers between devices with their start and end apart: 2 -> 0, of which waited for: 2 -> 0; matrix products, arithmetic and copies ran while one was open for 3% -> 0% of each run, Pallas kernels for 0% -> 0%
where the time goes in v2:
time: 42.8 us; the launch traced here: 42.5 us
  Pallas kernels  35.3 us (82%)
  local copies, waits for them, and re-layouts  5.55 us (13%)
  other arithmetic  1.55 us (4%)
    pallas_call x1, Pallas kernels, on_device(): pl.pallas_call(functools.partial(kernel, (rows, cols, layers, rl, pg, cl,...  35.3 us
    unnamed x6, local copies, waits for them, and re-layouts  4.07 us
    lt x2, other arithmetic, slot_table(): live = slot < counts[..., None]  1.34 us

profile of v2, /device:TPU:0, one launch (start us, length us, event | category | flops | bytes accessed | tf_op | source)
XLA Modules:
  0.0 42.5 jit_solution(9194122391296712651)
XLA Ops:
  0.0 0.7 %iota_compare_fusion.3 = pred[4,6]{0,1:T(8,128)(4,1)S(1)} fusion(s32[4]{0:T(128)} %bitcast.15), kind=kLoop, calls=%fused_computation.7 | loop fusion | flops 24 | bytes 40 | tf_op jit(solution)/shard_map/lt | solution.py:18
  0.7 0.7 %iota_compare_fusion.2 = pred[2,8,6]{1,2,0:T(8,128)(4,1)S(1)} fusion(s32[2,8]{1,0:T(2,128)} %param.11), kind=kLoop, calls=%fused_computation.6 | loop fusion | flops 96 | bytes 160 | tf_op jit(solution)/shard_map/lt | solution.py:18
  1.4 0.8 %copy.14 = s32[4,6]{0,1:T(8,128)S(1)} copy(s32[4,6]{1,0:T(4,128)} %bitcast.14) | data formatting | bytes 192 | tf_op jit(solution)/shard_map/eq | solution.py:19
  2.1 0.1 select_reduce_fusion.1
  2.2 0.1 reshape.52
  2.3 0.1 broadcast_in_dim.42
  2.4 0.1 reshape.49
  2.5 0.7 %copy.18 = s32[2,8,6]{1,2,0:T(8,128)S(1)} copy(s32[2,8,6]{1,0,2:T(2,128)} %param.10) | data formatting | bytes 768 | tf_op args[4]
  3.2 0.1 select_reduce_fusion
  3.3 0.1 copy.19
  3.5 0.2 broadcast_in_dim.45
  3.7 0.1 reshape.51
  3.8 0.0 copy-start
  3.8 1.4 %copy-done = bf16[2,8,6,64,64]{4,3,2,1,0:T(8,128)(2,1)S(1)} copy-done((bf16[2,8,6,64,64]{4,3,2,1,0:T(8,128)(2,1)S(1)}, bf16[2,8,6,64,64]{4,3,2,1,0:T(8,128)(2,1)}, u32[]{:S(2)}) %copy-start) | copy-done | bytes 786456
  5.2 0.0 copy-start.1
  5.2 1.0 %copy-done.1 = bf16[4,1,6,64,64]{4,3,2,1,0:T(8,128)(2,1)S(1)} copy-done((bf16[4,1,6,64,64]{4,3,2,1,0:T(8,128)(2,1)S(1)}, bf16[4,1,6,64,64]{4,3,2,1,0:T(8,128)(2,1)}, u32[]{:S(2)}) %copy-start.1) | copy-done | bytes 196632
  6.2 35.3 %shard_map.67 = bf16[1024,512]{1,0:T(8,128)(2,1)S(1)} custom-call(bf16[4,6,64,64]{3,2,1,0:T(8,128)(2,1)S(1)} %bitcast.12, bf16[4,16,128]{2,1,0:T(8,128)(2,1)S(1)} %pad.8.ltab, bf16[16,6,64,64]{3,2,1,0:T(8,128)(2,1)S(1)} %bitcast.11, bf16[8,16,128]{2,1,0:T(8,128)(2,1)S(1)} %pad.9.rtab), custom_call_target="tpu_custom_call" | custom-call | flops 3221225472 | bytes 1048576 | tf_op jit(solution)/shard_map/pallas_call | solution.py:265
  41.5 1.0 %copy.24 = bf16[1024,512]{1,0:T(8,128)(2,1)} copy(bf16[1024,512]{1,0:T(8,128)(2,1)S(1)} %shard_map.67) | data formatting | bytes 2097152
  (8 shorter events, 0.1 us)
Async XLA Ops:
  3.8 1.4 %copy-start = (bf16[2,8,6,64,64]{4,3,2,1,0:T(8,128)(2,1)S(1)}, bf16[2,8,6,64,64]{4,3,2,1,0:T(8,128)(2,1)}, u32[]{:S(2)}) copy-start(bf16[2,8,6,64,64]{4,3,2,1,0:T(8,128)(2,1)} %param.9) | copy-start | bytes 2359300
  5.2 1.0 %copy-start.1 = (bf16[4,1,6,64,64]{4,3,2,1,0:T(8,128)(2,1)S(1)}, bf16[4,1,6,64,64]{4,3,2,1,0:T(8,128)(2,1)}, u32[]{:S(2)}) copy-start(bf16[4,1,6,64,64]{4,3,2,1,0:T(8,128)(2,1)} %param.6) | copy-start | bytes 589828

commit v3 on v2

v3 whole, which is shorter than its diff:
```python
import functools

import jax
import jax.numpy as jnp
from jax import lax
from jax.experimental import pallas as pl
from jax.experimental.pallas import tpu as pltpu
from jax.sharding import PartitionSpec as P

KP = 12
MESH = pl.DeviceIdType.MESH
TAB = 16
LAG = 2
VMEM_LIMIT = 251 * 256 * 1024


def partner(index, bit):
    return index + bit - 2 * bit * ((index // bit) % 2)


def bits_of(size):
    bits = []
    while size > 1:
        size //= 2
        bits.append(size)
    return bits


def moved(index, e, bits):
    for bit in bits:
        if e & bit:
            index = partner(index, bit)
    return index


def lower_bits(e, bits):
    return [n for n, bit in enumerate(bits) if e == 0 or bit < (e & -e)]


def placed(tabs, want, parts):
    outs = [jnp.zeros_like(part) for part in parts[0]]
    for tab, part in zip(tabs, parts):
        mask = tab == want
        outs = [jnp.where(mask, new, old) for new, old in zip(part, outs)]
    return outs


def spread_rows(tab, slots):
    return [jnp.broadcast_to(tab[s : s + 1, :], tab.shape) for s in range(slots)]


def kernel(dims, lpos, lcnt, rpos, rcnt, lhbm, rhbm, out_ref, lblk, rblk, lbuf, rbuf, ld, rd, insem, lsend, lrecv, rsend, rrecv):
    rows, cols, layers, rl, pg, cl, slots, side = dims
    half = side // 2
    width = 2 * side
    r, c, d = lax.axis_index("row"), lax.axis_index("col"), lax.axis_index("depth")
    lbits, rbits = bits_of(layers), bits_of(rows)
    chunks = pg * cl // 2
    me = c * layers + d
    parts_of = 2 if rl % 2 == 0 else 1
    pl_rows = rl // parts_of

    left_in = pltpu.make_async_copy(lhbm, lblk, insem.at[chunks])
    left_in.start()

    def right_in(chunk):
        at = pl.ds(2 * chunk, 2)
        return pltpu.make_async_copy(rhbm.at[at], rblk.at[at], insem.at[chunk])

    for chunk in range(chunks):
        right_in(chunk).start()

    lane = lax.broadcasted_iota(jnp.int32, (TAB, width), 1)
    line = lax.broadcasted_iota(jnp.int32, (TAB, width), 0)

    def shown(position, count, s):
        return jnp.where(s < count, position, KP)

    barrier = pltpu.get_barrier_semaphore()
    peers = [{"depth": partner(d, bit)} for bit in lbits] + [{"row": partner(r, bit)} for bit in rbits]
    if cols > 1:
        peers += [{"col": lax.rem(c + 1, cols)}, {"col": lax.rem(c + cols - 1, cols)}]
    for peer in peers:
        pl.semaphore_signal(barrier, inc=1, device_id=peer, device_id_type=MESH)

    left_in.wait()

    def pack_left(i, carry):
        tab = jnp.full((TAB, width), KP, jnp.int32)
        for s in range(slots):
            x = lblk[i, s]
            lbuf[me, i, s * half : (s + 1) * half, :] = jnp.concatenate([x[:half], x[half:]], axis=1)
            tab = jnp.where(line == s, shown(lpos[i, s], lcnt[i], s), tab)
        lbuf[me, i, slots * half : slots * half + TAB, :] = tab.astype(jnp.float32).astype(jnp.bfloat16)
        return carry

    lax.fori_loop(0, rl, pack_left, 0)
    pl.semaphore_wait(barrier, len(peers))

    def left_copy(way, owner, h, device):
        piece = lbuf.at[owner, pl.ds(h * pl_rows, pl_rows)]
        return pltpu.make_async_remote_copy(
            src_ref=piece,
            dst_ref=piece,
            send_sem=lsend.at[way, owner, h],
            recv_sem=lrecv.at[owner, h],
            device_id=device,
            device_id_type=MESH,
        )

    def left_sends(t, h, side_of, e, act):
        src = c + t if side_of else c - t
        owner = src * layers + moved(d, e, lbits)
        if e == 0:
            if side_of == 0:
                @pl.when(c + 1 < cols)
                def _():
                    act(left_copy(0, owner, h, {"col": c + 1}))

            def to_lower():
                act(left_copy(1, owner, h, {"col": c - 1}))

            if side_of == 1:
                pl.when(c > 0)(to_lower)
            else:
                pl.when((c > 0) & (t == 0))(to_lower)
        for n in lower_bits(e, lbits):
            act(left_copy(2 + n, owner, h, {"depth": partner(d, lbits[n])}))

    def valid(t, side_of):
        if side_of:
            return (t > 0) & (c + t < cols)
        return (t >= 0) & (c - t >= 0)

    for h in range(parts_of):
        left_sends(0, h, 0, 0, lambda copy: copy.start())

    def right_copy(n, owner, chunk):
        return pltpu.make_async_remote_copy(
            src_ref=rbuf.at[owner, chunk],
            dst_ref=rbuf.at[owner, chunk],
            send_sem=rsend.at[n, owner, chunk],
            recv_sem=rrecv.at[owner, chunk],
            device_id={"row": partner(r, rbits[n])},
            device_id_type=MESH,
        )

    def pack_right(chunk, carry):
        right_in(chunk).wait()
        tab = jnp.full((TAB, width), KP, jnp.int32)
        g, j = chunk // (cl // 2), 2 * (chunk % (cl // 2))
        for s in range(slots):
            first = shown(rpos[s, g, j], rcnt[g, j], s)
            second = shown(rpos[s, g, j + 1], rcnt[g, j + 1], s)
            tab = jnp.where(line == s, jnp.where(lane < side, first, second), tab)
            rbuf[r, chunk, s * side : (s + 1) * side, :] = jnp.concatenate(
                [rblk[2 * chunk, s], rblk[2 * chunk + 1, s]], axis=1
            )
        rbuf[r, chunk, slots * side : slots * side + TAB, :] = tab.astype(jnp.float32).astype(jnp.bfloat16)
        for n in lower_bits(0, rbits):
            right_copy(n, r, chunk).start()
        return carry

    lax.fori_loop(0, chunks, pack_right, 0)

    def place_right(owner, chunk):
        g = owner * pg + chunk // (cl // 2)
        lanes = pl.ds(pl.multiple_of((chunk % (cl // 2)) * width, width), width)
        tabs = spread_rows(rbuf[owner, chunk, slots * side : slots * side + TAB, :], slots)
        for v in range(side // TAB):
            parts = [(rbuf[owner, chunk, s * side + v * TAB : s * side + (v + 1) * TAB, :],) for s in range(slots)]
            for p in range(KP):
                (block,) = placed(tabs, jnp.asarray(p, jnp.bfloat16), parts)
                rd[pl.ds(pl.multiple_of((g * KP + p) * side + v * TAB, TAB), TAB), lanes] = block

    upper = (lane >= side).astype(jnp.float32).astype(jnp.bfloat16)

    def place_left(src, layer, h):
        owner = src * layers + layer

        def one(i, carry):
            base = (layer * rl + i) * side
            tabs = spread_rows(lbuf[owner, i, slots * half : slots * half + TAB, :], slots)
            for v in range(half // TAB):
                parts = []
                for s in range(slots):
                    x = lbuf[owner, i, s * half + v * TAB : s * half + (v + 1) * TAB, :]
                    lo, hi = x[:, :side], x[:, side:]
                    parts.append((jnp.concatenate([lo, lo], axis=1), jnp.concatenate([hi, hi], axis=1)))
                for q in range(KP // 2):
                    top, bottom = placed(tabs, upper + jnp.asarray(2 * q, jnp.bfloat16), parts)
                    lanes = pl.ds(pl.multiple_of((src * (KP // 2) + q) * width, width), width)
                    ld[pl.ds(pl.multiple_of(base + v * TAB, TAB), TAB), lanes] = top
                    ld[pl.ds(pl.multiple_of(base + half + v * TAB, TAB), TAB), lanes] = bottom
            return carry

        lax.fori_loop(h * pl_rows, (h + 1) * pl_rows, one, 0)

    def own_right(chunk, carry):
        place_right(r, chunk)
        return carry

    lax.fori_loop(0, chunks, own_right, 0)

    order = sorted(range(layers), key=lambda e: (e.bit_count(), -e))
    last = max(e.bit_count() for e in order)

    def left_step(u, carry):
        t, h = u // parts_of, u % parts_of
        for e in order:
            lag = e.bit_count()
            for side_of in (0, 1):
                tt = t - lag

                @pl.when(valid(tt, side_of) & (tt < cols))
                def _(tt=tt, e=e, side_of=side_of):
                    src = c + tt if side_of else c - tt
                    layer = moved(d, e, lbits)

                    def arrive():
                        left_copy(0, src * layers + layer, h, {"depth": partner(d, 1)}).wait_recv()
                        left_sends(tt, h, side_of, e, lambda copy: copy.start())

                    if e == 0:
                        pl.when(tt > 0)(arrive)
                    else:
                        arrive()
                    place_left(src, layer, h)
        return carry

    def right_arrive(e, chunk):
        owner = moved(r, e, rbits)
        right_copy(0, owner, chunk).wait_recv()
        for n in lower_bits(e, rbits):
            right_copy(n, owner, chunk).start()
        place_right(owner, chunk)

    arrivals = sorted(range(1, rows), key=lambda e: (e.bit_count(), -e))
    steps = (cols + last - 1) * parts_of
    paired = rows == 2 and cols > 1

    def share(u):
        return jnp.clip(chunks * (u - LAG) // (steps - 1 - LAG), 0, chunks)

    def both_step(u, carry):
        left_step(u, carry)
        if paired:

            def one(chunk, carry):
                right_arrive(1, chunk)
                return carry

            lax.fori_loop(share(u - 1), share(u), one, 0)
        return carry

    lax.fori_loop(0, steps, both_step, 0)
    if not paired:
        for e in arrivals:

            def one(chunk, carry, e=e):
                right_arrive(e, chunk)
                return carry

            lax.fori_loop(0, chunks, one, 0)

    tile = rl * side

    def multiply(layer):
        at = pl.ds(pl.multiple_of(layer * tile, tile), tile)
        out_ref[at, :] = jnp.dot(ld[at, :], rd[...], preferred_element_type=jnp.float32).astype(jnp.bfloat16)

    early = [e for e in order if e.bit_count() < last or last == 0]
    late = [e for e in order if e not in early]

    def multiply_all(group):
        def one(n, carry):
            multiply(lax.rem(d + n, layers))
            return carry

        if len(group) == layers:
            lax.fori_loop(0, layers, one, 0)
        else:
            first = moved(d, late[0], lbits) if late else d

            def other(n, carry):
                multiply(lax.rem(first + 1 + n, layers))
                return carry

            if group is early:
                lax.fori_loop(0, layers - 1, other, 0)
            else:
                multiply(first)

    multiply_all(early)
    lax.fori_loop(steps, steps + parts_of, left_step, 0)
    if late:
        multiply_all(late)

    def left_done(u, carry):
        t, h = u // parts_of, u % parts_of
        for e in range(layers):
            for side_of in (0, 1):

                @pl.when(valid(t, side_of))
                def _(e=e, side_of=side_of):
                    left_sends(t, h, side_of, e, lambda copy: copy.wait_send())

        return carry

    lax.fori_loop(0, cols * parts_of, left_done, 0)
    for e in range(rows):
        owner = moved(r, e, rbits)

        def right_done(chunk, carry, owner=owner, e=e):
            for n in lower_bits(e, rbits):
                right_copy(n, owner, chunk).wait_send()
            return carry

        lax.fori_loop(0, chunks, right_done, 0)


def on_device(row_blocks, row_positions, row_counts, col_blocks, col_positions, col_counts):
    rows, cols, layers = lax.axis_size("row"), lax.axis_size("col"), lax.axis_size("depth")
    rl, _, slots, side, _ = row_blocks.shape
    pg, cl = col_blocks.shape[:2]
    panels = pg * rows
    chunks = pg * cl // 2
    m, n, k = layers * rl * side, cl * side, panels * KP * side
    width = 2 * side
    vmem = pl.BlockSpec(memory_space=pltpu.VMEM)
    smem = pl.BlockSpec(memory_space=pltpu.SMEM)
    hbm = pl.BlockSpec(memory_space=pltpu.HBM)
    return pl.pallas_call(
        functools.partial(kernel, (rows, cols, layers, rl, pg, cl, slots, side)),
        out_shape=jax.ShapeDtypeStruct((m, n), jnp.bfloat16),
        in_specs=[smem] * 4 + [hbm] * 2,
        out_specs=vmem,
        scratch_shapes=[
            pltpu.VMEM((rl, slots, side, side), jnp.bfloat16),
            pltpu.VMEM((pg * cl, slots, side, side), jnp.bfloat16),
            pltpu.VMEM((cols * layers, rl, slots * side // 2 + TAB, width), jnp.bfloat16),
            pltpu.VMEM((rows, chunks, slots * side + TAB, width), jnp.bfloat16),
            pltpu.VMEM((m, k), jnp.bfloat16),
            pltpu.VMEM((k, n), jnp.bfloat16),
            pltpu.SemaphoreType.DMA((chunks + 1,)),
            pltpu.SemaphoreType.DMA((2 + len(bits_of(layers)), cols * layers, 2)),
            pltpu.SemaphoreType.DMA((cols * layers, 2)),
            pltpu.SemaphoreType.DMA((len(bits_of(rows)), rows, chunks)),
            pltpu.SemaphoreType.DMA((rows, chunks)),
        ],
        compiler_params=pltpu.CompilerParams(
            collective_id=0, has_side_effects=True, vmem_limit_bytes=VMEM_LIMIT
        ),
        cost_estimate=pl.CostEstimate(flops=2 * m * n * k, bytes_accessed=2 * m * n, transcendentals=0),
    )(
        row_positions[:, 0],
        row_counts[:, 0],
        col_positions.transpose(2, 0, 1),
        col_counts,
        row_blocks[:, 0],
        col_blocks.reshape(pg * cl, slots, side, side),
    )


def solution(mesh):
    in_specs = (
        P(("row", "depth"), "col", None, None, None),
        P(("row", "depth"), "col", None),
        P(("row", "depth"), "col"),
        P("row", ("col", "depth"), None, None, None),
        P("row", ("col", "depth"), None),
        P("row", ("col", "depth")),
    )
    return jax.shard_map(
        on_device, mesh=mesh, in_specs=in_specs, out_specs=P("row", ("col", "depth")), check_vma=False
    )
```

time: 42.8 us -> 37.6 us (0.88)
  local copies, waits for them, and re-layouts: 5.55 us -> 2.26 us
  other arithmetic: 1.55 us -> 0 us
    unnamed x6 -> x1, local copies, waits for them, and re-layouts: 4.07 us -> 2.26 us
    lt x2 -> x0, other arithmetic: 1.34 us -> none  [slot_table(): live = slot < counts[..., None]]
    eq x1 -> x0, local copies, waits for them, and re-layouts: 0.77 us -> none  [slot_table(): positions[..., :, None] == jnp.arange(KP, dtype=jnp.int32)]
where the time goes in v3:
time: 37.6 us; the launch traced here: 37.3 us
  Pallas kernels  35.1 us (93%)
  local copies, waits for them, and re-layouts  2.26 us (6%)
    pallas_call x1, Pallas kernels, on_device(): pl.pallas_call(functools.partial(kernel, (rows, cols, layers, rl, pg, cl,...  35.1 us
    unnamed x1, local copies, waits for them, and re-layouts  2.26 us

profile of v3, /device:TPU:0, one launch (start us, length us, event | category | flops | bytes accessed | tf_op | source)
XLA Modules:
  0.0 37.3 jit_solution(17144005230717396381)
XLA Ops:
  0.0 35.1 %shard_map.64 = bf16[1024,512]{1,0:T(8,128)(2,1)} custom-call(s32[4,6]{1,0:T(4,128)} %bitcast.8, s32[4]{0:T(128)} %bitcast.9, s32[6,2,8]{2,1,0:T(2,128)} %bitcast.7, s32[2,8]{1,0:T(2,128)} %rcnt.1, bf16[4,6,64,64]{3,2,1,0:T(8,128)(2,1)} %bitcast.6, bf16[16,6,64,64]{3,2,1,0:T(8,128)(2,1)} %bitcast.5), custom_call_target="tpu_custom_call" | custom-call | flops 3221225472 | bytes 1048576 | tf_op jit(solution)/shard_map/pallas_call | solution.py:333
  35.1 2.3 %copy.8 = bf16[1024,512]{1,0:T(8,128)(2,1)} copy(bf16[1024,512]{1,0:T(8,128)(2,1)} %shard_map.64) | data formatting | bytes 2097152

commit v4 on v3

--- a/solution.py
+++ b/solution.py
@@ -49,7 +49,7 @@
     return [jnp.broadcast_to(tab[s : s + 1, :], tab.shape) for s in range(slots)]
 
 
-def kernel(dims, lpos, lcnt, rpos, rcnt, lhbm, rhbm, out_ref, lblk, rblk, lbuf, rbuf, ld, rd, insem, lsend, lrecv, rsend, rrecv):
+def kernel(dims, lpos, lcnt, rpos, rcnt, lhbm, rhbm, out_ref, lblk, rblk, lbuf, rbuf, ld, rd, acc, insem, lsend, lrecv, rsend, rrecv):
     rows, cols, layers, rl, pg, cl, slots, side = dims
     half = side // 2
     width = 2 * side
@@ -57,8 +57,9 @@
     lbits, rbits = bits_of(layers), bits_of(rows)
     chunks = pg * cl // 2
     me = c * layers + d
-    parts_of = 2 if rl % 2 == 0 else 1
+    parts_of = 2
     pl_rows = rl // parts_of
+    body = slots * half
 
     left_in = pltpu.make_async_copy(lhbm, lblk, insem.at[chunks])
     left_in.start()
@@ -85,20 +86,23 @@
 
     left_in.wait()
 
-    def pack_left(i, carry):
+    def pack_left(h, carry):
         tab = jnp.full((TAB, width), KP, jnp.int32)
-        for s in range(slots):
-            x = lblk[i, s]
-            lbuf[me, i, s * half : (s + 1) * half, :] = jnp.concatenate([x[:half], x[half:]], axis=1)
-            tab = jnp.where(line == s, shown(lpos[i, s], lcnt[i], s), tab)
-        lbuf[me, i, slots * half : slots * half + TAB, :] = tab.astype(jnp.float32).astype(jnp.bfloat16)
-        return carry
-
-    lax.fori_loop(0, rl, pack_left, 0)
+        for i2 in range(pl_rows):
+            i = h * pl_rows + i2
+            for s in range(slots):
+                x = lblk[i, s]
+                at = i2 * body + s * half
+                lbuf[me, h, at : at + half, :] = jnp.concatenate([x[:half], x[half:]], axis=1)
+                tab = jnp.where(line == i2 * slots + s, shown(lpos[i, s], lcnt[i], s), tab)
+        lbuf[me, h, pl_rows * body :, :] = tab.astype(jnp.float32).astype(jnp.bfloat16)
+        return carry
+
+    lax.fori_loop(0, parts_of, pack_left, 0)
     pl.semaphore_wait(barrier, len(peers))
 
     def left_copy(way, owner, h, device):
-        piece = lbuf.at[owner, pl.ds(h * pl_rows, pl_rows)]
+        piece = lbuf.at[owner, h]
         return pltpu.make_async_remote_copy(
             src_ref=piece,
             dst_ref=piece,
@@ -178,29 +182,33 @@
     def place_left(src, layer, h):
         owner = src * layers + layer
 
-        def one(i, carry):
-            base = (layer * rl + i) * side
-            tabs = spread_rows(lbuf[owner, i, slots * half : slots * half + TAB, :], slots)
+        tabs = spread_rows(lbuf[owner, h, pl_rows * body :, :], pl_rows * slots)
+        for i2 in range(pl_rows):
+            base = (layer * rl + h * pl_rows + i2) * side
+            mine = tabs[i2 * slots : (i2 + 1) * slots]
             for v in range(half // TAB):
                 parts = []
                 for s in range(slots):
-                    x = lbuf[owner, i, s * half + v * TAB : s * half + (v + 1) * TAB, :]
+                    at = i2 * body + s * half + v * TAB
+                    x = lbuf[owner, h, at : at + TAB, :]
                     lo, hi = x[:, :side], x[:, side:]
                     parts.append((jnp.concatenate([lo, lo], axis=1), jnp.concatenate([hi, hi], axis=1)))
                 for q in range(KP // 2):
-                    top, bottom = placed(tabs, upper + jnp.asarray(2 * q, jnp.bfloat16), parts)
+                    top, bottom = placed(mine, upper + jnp.asarray(2 * q, jnp.bfloat16), parts)
                     lanes = pl.ds(pl.multiple_of((src * (KP // 2) + q) * width, width), width)
                     ld[pl.ds(pl.multiple_of(base + v * TAB, TAB), TAB), lanes] = top
                     ld[pl.ds(pl.multiple_of(base + half + v * TAB, TAB), TAB), lanes] = bottom
-            return carry
-
-        lax.fori_loop(h * pl_rows, (h + 1) * pl_rows, one, 0)
 
     def own_right(chunk, carry):
         place_right(r, chunk)
         return carry
 
     lax.fori_loop(0, chunks, own_right, 0)
+
+    tile = rl * side
+    paired = rows == 2 and cols > 1
+    if paired:
+        acc[...] = jnp.zeros_like(acc)
 
     order = sorted(range(layers), key=lambda e: (e.bit_count(), -e))
     last = max(e.bit_count() for e in order)
@@ -226,6 +234,14 @@
                     else:
                         arrive()
                     place_left(src, layer, h)
+                    if paired:
+
+                        @pl.when((src // pg == r) & (h == parts_of - 1))
+                        def _():
+                            at = pl.ds(pl.multiple_of(layer * tile, tile), tile)
+                            inner = pl.ds(pl.multiple_of(src * KP * side, KP * side), KP * side)
+                            acc[at, :] += jnp.dot(ld[at, inner], rd[inner, :], preferred_element_type=jnp.float32)
+
         return carry
 
     def right_arrive(e, chunk):
@@ -237,7 +253,6 @@
 
     arrivals = sorted(range(1, rows), key=lambda e: (e.bit_count(), -e))
     steps = (cols + last - 1) * parts_of
-    paired = rows == 2 and cols > 1
 
     def share(u):
         return jnp.clip(chunks * (u - LAG) // (steps - 1 - LAG), 0, chunks)
@@ -263,11 +278,15 @@
 
             lax.fori_loop(0, chunks, one, 0)
 
-    tile = rl * side
-
     def multiply(layer):
         at = pl.ds(pl.multiple_of(layer * tile, tile), tile)
-        out_ref[at, :] = jnp.dot(ld[at, :], rd[...], preferred_element_type=jnp.float32).astype(jnp.bfloat16)
+        if paired:
+            size = pg * KP * side
+            inner = pl.ds(pl.multiple_of((1 - r) * size, size), size)
+            total = acc[at, :] + jnp.dot(ld[at, inner], rd[inner, :], preferred_element_type=jnp.float32)
+        else:
+            total = jnp.dot(ld[at, :], rd[...], preferred_element_type=jnp.float32)
+        out_ref[at, :] = total.astype(jnp.bfloat16)
 
     early = [e for e in order if e.bit_count() < last or last == 0]
     late = [e for e in order if e not in early]
@@ -338,10 +357,11 @@
         scratch_shapes=[
             pltpu.VMEM((rl, slots, side, side), jnp.bfloat16),
             pltpu.VMEM((pg * cl, slots, side, side), jnp.bfloat16),
-            pltpu.VMEM((cols * layers, rl, slots * side // 2 + TAB, width), jnp.bfloat16),
+            pltpu.VMEM((cols * layers, 2, rl // 2 * slots * side // 2 + TAB, width), jnp.bfloat16),
             pltpu.VMEM((rows, chunks, slots * side + TAB, width), jnp.bfloat16),
             pltpu.VMEM((m, k), jnp.bfloat16),
             pltpu.VMEM((k, n), jnp.bfloat16),
+            pltpu.VMEM((m if rows == 2 else 8, n), jnp.float32),
             pltpu.SemaphoreType.DMA((chunks + 1,)),
             pltpu.SemaphoreType.DMA((2 + len(bits_of(layers)), cols * layers, 2)),
             pltpu.SemaphoreType.DMA((cols * layers, 2)),

time: 37.6 us -> 34.9 us (0.928)
  Pallas kernels: 35.1 us -> 32.4 us
    pallas_call x1, Pallas kernels: 35.1 us -> 32.4 us  [on_device(): pl.pallas_call(functools.partial(kernel, (rows, cols, layers, rl, pg, cl,...]
where the time goes in v4:
time: 34.9 us; the launch traced here: 34.7 us
  Pallas kernels  32.4 us (93%)
  local copies, waits for them, and re-layouts  2.26 us (6%)
    pallas_call x1, Pallas kernels, on_device(): pl.pallas_call(functools.partial(kernel, (rows, cols, layers, rl, pg, cl,...  32.4 us
    unnamed x1, local copies, waits for them, and re-layouts  2.26 us

profile of v4, /device:TPU:0, one launch (start us, length us, event | category | flops | bytes accessed | tf_op | source)
XLA Modules:
  0.0 34.7 jit_solution(11773444942165482691)
XLA Ops:
  0.0 32.4 %shard_map.64 = bf16[1024,512]{1,0:T(8,128)(2,1)} custom-call(s32[4,6]{1,0:T(4,128)} %bitcast.8, s32[4]{0:T(128)} %bitcast.9, s32[6,2,8]{2,1,0:T(2,128)} %bitcast.7, s32[2,8]{1,0:T(2,128)} %rcnt.1, bf16[4,6,64,64]{3,2,1,0:T(8,128)(2,1)} %bitcast.6, bf16[16,6,64,64]{3,2,1,0:T(8,128)(2,1)} %bitcast.5), custom_call_target="tpu_custom_call" | custom-call | flops 3221225472 | bytes 1048576 | tf_op jit(solution)/shard_map/pallas_call | solution.py:352
  32.4 2.3 %copy.8 = bf16[1024,512]{1,0:T(8,128)(2,1)} copy(bf16[1024,512]{1,0:T(8,128)(2,1)} %shard_map.64) | data formatting | bytes 2097152
